TPU v7x, 512 devices: a whole 4x8x8 slice. The times are simulated.
512 devices in a mesh: dom: 4 (over x), tp: 32 (over z_hi, y, core), dp: 4 (over z_lo).
Axes of the slice: x: 4, y: 8, z: 8 (z_hi: 2, z_lo: 4; z = z_hi * 4 + z_lo), core: 2. Of those that a mesh axis runs over, the one named last changes fastest.
Arguments:
- query: bfloat16 [32, 16, 8192], P('tp'), may hold values from -12 to 12
- key_block_pool: bfloat16 [32, 8192, 1024], P('tp', ('dom', 'dp')), may hold values from -6 to 6
- value_block_pool: bfloat16 [32, 8192, 1024], P('tp', ('dom', 'dp')), may hold values from -12 to 12
- row_blocks: int32 [32, 16], P('tp'), may hold values from 1 to 32, 64 in all within a row
- trim: int32 [32, 16], P('tp'), may hold values from 0 to 127
- ffn_in: bfloat16 [256, 8192], P('tp', ('dom', 'dp')), may hold values from -6 to 6
- w_gate: bfloat16 [8192, 28672], P(('dom', 'dp'), 'tp'), may hold values from -0.0625 to 0.0625
- w_up: bfloat16 [8192, 28672], P(('dom', 'dp'), 'tp'), may hold values from -0.0625 to 0.0625
- w_down: bfloat16 [28672, 8192], P('tp', ('dom', 'dp')), may hold values from -0.03125 to 0.03125
Outputs:
- attn_out: bfloat16 [32, 16, 8192], P('tp', None, ('dom', 'dp'))
- ffn_out: bfloat16 [256, 8192], P('tp', ('dom', 'dp'))
Inputs may be any that keep to these rules, and one draw needn't show every extreme that they name: `row_blocks`: each attention row holds 1 to 32 blocks; the 16 rows of one row group (one line of the array) together fill its pool of 64 blocks exactly, and some row holds 32 blocks.
All inputs are finite; a program needn't handle non-finite values.
Results may differ from a plain program's by a relative error of at most 0.006.
Values may be sent and summed in bfloat16 or wider, within the bound.
A program may use at most 64 MiB of HBM per device.

v0:
```python
import jax
import jax.numpy as jnp
from jax import lax
from jax.sharding import PartitionSpec as P

QUERY_HEADS = 64
KEY_HEADS = 8
HEAD_SIZE = 128
BLOCK_POSITIONS = 128


NEG = -1e30


def attention_part(query, key_block_pool, value_block_pool, row_blocks, trim):
    rows = query.shape[1]
    block_count = key_block_pool.shape[1] // BLOCK_POSITIONS
    row_group = QUERY_HEADS // KEY_HEADS
    counts = row_blocks[0]
    trims = trim[0]
    starts = jnp.cumsum(counts) - counts
    index = lax.axis_index(("dom", "dp")) * block_count + jnp.arange(block_count, dtype=jnp.int32)
    block_row_index = jnp.sum((starts[None, :] <= index[:, None]).astype(jnp.int32), axis=1) - 1
    onehot = block_row_index[:, None] == jnp.arange(rows, dtype=jnp.int32)[None, :]
    sel_int = onehot.astype(jnp.int32)
    sel_start = jnp.sum(sel_int * starts[None, :], axis=1)
    sel_count = jnp.sum(sel_int * counts[None, :], axis=1)
    sel_trim = jnp.sum(sel_int * trims[None, :], axis=1)
    last = index - sel_start == sel_count - 1
    cache_cells = jnp.arange(BLOCK_POSITIONS, dtype=jnp.int32)
    live = jnp.logical_or(
        jnp.logical_not(last)[:, None], cache_cells[None, :] < (BLOCK_POSITIONS - sel_trim)[:, None]
    )
    chosen_blocks = jnp.dot(
        onehot.astype(jnp.bfloat16), query[0], preferred_element_type=jnp.float32
    ).astype(jnp.bfloat16)
    query_block = chosen_blocks.reshape(block_count, KEY_HEADS, row_group, HEAD_SIZE)
    key_block = key_block_pool[0].reshape(block_count, BLOCK_POSITIONS, KEY_HEADS, HEAD_SIZE)
    value_block = value_block_pool[0].reshape(block_count, BLOCK_POSITIONS, KEY_HEADS, HEAD_SIZE)
    scores = jnp.einsum(
        "bkgd,btkd->bkgt", query_block, key_block, preferred_element_type=jnp.float32
    ) * HEAD_SIZE ** (-0.5)
    scores = jnp.where(live[:, None, None, :], scores, NEG)
    bmax = jnp.max(scores, axis=3)
    local_top = jnp.max(jnp.where(onehot[:, :, None, None], bmax[:, None], NEG), axis=0)
    top = lax.pmax(local_top, ("dom", "dp"))
    sel = onehot.astype(jnp.float32)
    block_top = jnp.dot(
        sel, top.reshape(rows, QUERY_HEADS), precision=lax.Precision.HIGHEST
    ).reshape(block_count, KEY_HEADS, row_group)
    weights = jnp.exp(scores - block_top[..., None]).astype(jnp.bfloat16)
    den_b = jnp.sum(weights.astype(jnp.float32), axis=3)
    num_b = jnp.einsum("bkgt,btkd->bkgd", weights, value_block, preferred_element_type=jnp.float32)
    numer = jnp.einsum(
        "br,bx->rx",
        sel,
        num_b.reshape(block_count, QUERY_HEADS * HEAD_SIZE),
        precision=lax.Precision.HIGHEST,
    )
    total = jnp.einsum(
        "br,bx->rx", sel, den_b.reshape(block_count, QUERY_HEADS), precision=lax.Precision.HIGHEST
    )
    num_share, den_share = (
        lax.psum_scatter(numer, ("dom", "dp"), scatter_dimension=1, tiled=True),
        lax.psum_scatter(total, ("dom", "dp"), scatter_dimension=1, tiled=True),
    )
    heads_here = den_share.shape[1]
    result = num_share.reshape(rows, heads_here, HEAD_SIZE) / den_share[..., None]
    return result.reshape(1, rows, heads_here * HEAD_SIZE).astype(jnp.bfloat16)


def ffn_part(ffn_in, w_gate, w_up, w_down):
    piece = lax.all_gather(ffn_in, "tp", axis=0, tiled=True)
    gate_rows = jnp.dot(piece, w_gate, preferred_element_type=jnp.float32)
    up_rows = jnp.dot(piece, w_up, preferred_element_type=jnp.float32)
    partial_sums = jnp.stack([gate_rows, up_rows])
    summed = lax.psum(partial_sums, ("dom", "dp"))
    hidden = (jax.nn.silu(summed[0]) * summed[1]).astype(jnp.bfloat16)
    mixed = lax.psum_scatter(
        jnp.dot(hidden, w_down, preferred_element_type=jnp.float32),
        "tp",
        scatter_dimension=0,
        tiled=True,
    )
    return mixed.astype(jnp.bfloat16)


def shards(query, key_block_pool, value_block_pool, row_blocks, trim, ffn_in, w_gate, w_up, w_down):
    attn_out = attention_part(query, key_block_pool, value_block_pool, row_blocks, trim)
    ffn_out = ffn_part(ffn_in, w_gate, w_up, w_down)
    return (attn_out, ffn_out)


def solution(mesh):
    in_specs = (
        P("tp", None, None),
        P("tp", ("dom", "dp"), None),
        P("tp", ("dom", "dp"), None),
        P("tp", None),
        P("tp", None),
        P("tp", ("dom", "dp")),
        P(("dom", "dp"), "tp"),
        P(("dom", "dp"), "tp"),
        P("tp", ("dom", "dp")),
    )
    out_specs = (P("tp", None, ("dom", "dp")), P("tp", ("dom", "dp")))
    return jax.shard_map(shards, mesh=mesh, in_specs=in_specs, out_specs=out_specs, check_vma=False)
```

profile of v0, /device:TPU:1, one launch (start us, length us, event | category | flops | bytes accessed | tf_op | source)
XLA Modules:
  0.0 460.4 jit_solution(14980585984443473734)
XLA Ops:
  7.2 60.9 %all_gather.3 = bf16[256,512]{1,0:T(8,128)(2,1)S(1)} all-gather(bf16[8,512]{1,0:T(8,128)(2,1)} %param.14), channel_id=1, replica_groups=mesh['dom'=4,'tp'=32,'dp'=4] {'tp'}, dimensions={0}, use_global_device_ids=true | all-gather | bytes 270336 | tf_op jit(solution)/shard_map/all_gather | solution.py:73
  68.1 0.4 convolution_bitcast_fusion
  68.5 0.4 convolution_bitcast_fusion.1
  69.0 1.3 pad_maximum_fusion
  70.4 0.6 copy-done.5
  71.5 0.2 fusion.1
  71.7 0.3 copy.24
  72.0 0.2 select_reduce_fusion.3
  72.3 0.7 fusion.21
  73.2 68.5 %pmax.7 = f32[8,8,16]{2,1,0:T(8,128)S(1)} all-reduce(f32[8,8,16]{2,1,0:T(8,128)S(1)} %bitcast.75), channel_id=1, replica_groups=mesh['dom'=4,'tp'=32,'dp'=4] {'dom','dp'}, use_global_device_ids=true, to_apply=%region_7.8 | all-reduce | flops 1024 | bytes 8192 | tf_op jit(solution)/shard_map/pmax | solution.py:46
  141.6 0.3 fusion.17
  142.0 0.3 copy.25
  142.3 0.4 convolution_bitcast_fusion.2
  142.7 1.3 fusion.9
  144.1 88.8 %all-reduce.3.cloned.1.call-done = f32[2,256,896]{2,1,0:T(8,128)} async-done(((f32[2,256,896]{2,1,0:T(8,128)}), f32[2,256,896]{2,1,0:T(8,128)}) %all-reduce.3.cloned.1.call-update) | async-done | bytes 1835024 | tf_op jit(solution)/shard_map/psum | solution.py:77
  232.9 2.8 fusion.6
  235.7 0.2 convert_reduce_fusion
  236.0 1.3 dynamic-slice
  237.9 0.2 fusion.20
  238.2 66.1 %all-reduce = f32[16,64]{0,1:T(8,128)S(1)} all-reduce(f32[16,64]{0,1:T(8,128)S(1)} %fusion.20), channel_id=3, replica_groups=mesh['dom'=4,'tp'=32,'dp'=4] {'dom','dp'}, use_global_device_ids=true, to_apply=%region_10.11.clone | all-reduce | flops 1024 | bytes 8192
  304.3 15.5 %reduce-scatter.3.cloned.1.call-done = f32[16,512]{1,0:T(8,128)} async-done(((f32[16,8192]{1,0:T(8,128)}), f32[16,512]{1,0:T(8,128)}) %reduce-scatter.3.cloned.1.call-update) | async-done | bytes 32784 | tf_op jit(solution)/shard_map/reduce_scatter | solution.py:64
  319.9 1.4 fusion.15
  321.3 131.2 %reduce-scatter.5.cloned.1.call-done = f32[8,512]{1,0:T(8,128)} async-done(((f32[256,512]{1,0:T(8,128)}), f32[8,512]{1,0:T(8,128)}) %reduce-scatter.5.cloned.1.call-update) | async-done | bytes 16400 | tf_op jit(solution)/shard_map/reduce_scatter | solution.py:79
  452.6 1.3 convert_element_type.34
  (36 shorter events, 1.1 us)
Async XLA Ops:
  7.2 60.9 %copy-start = (bf16[512,896]{1,0:T(8,128)(2,1)S(1)}, bf16[512,896]{1,0:T(8,128)(2,1)}, u32[]{:S(2)}) copy-start(bf16[512,896]{1,0:T(8,128)(2,1)} %param.16) | copy-start | bytes 2752516
  7.2 61.4 %copy-start.3 = (bf16[512,896]{1,0:T(8,128)(2,1)S(1)}, bf16[512,896]{1,0:T(8,128)(2,1)}, u32[]{:S(2)}) copy-start(bf16[512,896]{1,0:T(8,128)(2,1)} %param.15) | copy-start | bytes 2752516
  7.2 225.7 %all-reduce.3.cloned.1.call-start = ((), (), s32[]{:S(2)}) async-start(), calls=%async_computation.3 | async-start | bytes 3670016 | tf_op jit(solution)/shard_map/psum | solution.py:77
  70.3 0.7 copy-start.5
  70.3 1.1 copy-start.4
  70.3 1.4 copy-start.1
  70.3 1.7 copy-start.6
  70.4 249.5 %reduce-scatter.3.cloned.1.call-start = ((), (), s32[]{:S(2)}) async-start(), calls=%async_computation.2 | async-start | bytes 557056 | tf_op jit(solution)/shard_map/reduce_scatter | solution.py:64
  71.7 70.3 %copy-start.2 = (bf16[1,512,1024]{2,1,0:T(8,128)(2,1)S(1)}, bf16[1,512,1024]{2,1,0:T(8,128)(2,1)}, u32[]{:S(2)}) copy-start(bf16[1,512,1024]{2,1,0:T(8,128)(2,1)} %param.11) | copy-start | bytes 3145732
  142.3 90.6 %copy-start.7 = (bf16[896,512]{1,0:T(8,128)(2,1)S(1)}, bf16[896,512]{1,0:T(8,128)(2,1)}, u32[]{:S(2)}) copy-start(bf16[896,512]{1,0:T(8,128)(2,1)} %param.17) | copy-start | bytes 2752516
  144.1 308.5 %reduce-scatter.5.cloned.1.call-start = ((), (), s32[]{:S(2)}) async-start(), calls=%async_computation.4 | async-start | bytes 540672 | tf_op jit(solution)/shard_map/reduce_scatter | solution.py:79
Sparse Core Ops, SparseCore 0:
  70.5 162.3 all-reduce.2
  235.9 83.8 reduce-scatter.2
  324.4 128.0 reduce-scatter.4
where the time goes:
time: 465 us; the launch traced here: 460 us
  waiting for transfers between devices  236 us (51%)
  blocking collectives  195 us (42%)
  between operations  14.6 us (3%)
  matrix products  6.92 us (1%)
  other arithmetic  5.14 us (1%)
    reduce_scatter x1, waiting for transfers between devices, ffn_part(): lax.psum_scatter(jnp.dot(hidden, w_down, preferred_element_type=jnp.float...  131 us
    psum x1, waiting for transfers between devices, ffn_part(): summed = lax.psum(partial_sums, ('dom', 'dp'))  88.8 us
    pmax x1, blocking collectives, attention_part(): top = lax.pmax(local_top, ('dom', 'dp'))  68.5 us
    unnamed x1, blocking collectives  66.1 us
    all_gather x1, blocking collectives, ffn_part(): piece = lax.all_gather(ffn_in, 'tp', axis=0, tiled=True)  60.9 us
    reduce_scatter x1, waiting for transfers between devices, attention_part(): lax.psum_scatter(numer, ('dom', 'dp'), scatter_dimension=1, tiled=True)  15.5 us
  transfers between devices with their start and end apart: 3, of which 3 were waited for; matrix products, arithmetic and copies ran while one was open for 2% of the time, Pallas kernels for 0%

commit v1 on v0

v1 whole, which is shorter than its diff:
```python
import jax
import jax.numpy as jnp
from jax import lax
from jax.experimental import pallas as pl
from jax.experimental.pallas import tpu as pltpu
from jax.sharding import PartitionSpec as P

QUERY_HEADS = 64
KEY_HEADS = 8
HEAD_SIZE = 128
NEG = -1e30
MESH = pl.DeviceIdType.MESH
F32 = jnp.float32
BF16 = jnp.bfloat16

PLANE = [(i, j) for i in range(4) for j in range(4) if i or j]
CHIPS = [(i, j) for i in range(2) for j in range(8) if i or j]


def iota(shape, axis):
    return lax.broadcasted_iota(jnp.int32, shape, axis)


def fold(rows):
    return jnp.concatenate([rows[:, :256], rows[:, 256:]], axis=0)


def unfold(piece):
    return jnp.concatenate([piece[:8], piece[8:]], axis=1)


def kernel(
    q_hbm, k_hbm, v_hbm, count_ref, trim_ref, rows_ref, wg_hbm, wu_hbm, wd_hbm,
    attn_ref, ffn_ref,
    q, k, v, wg, wu, wd,
    xp, xmat, psend, xr, zsend, zr, hall, ysend, yr, fsend, fr, asend, ar,
    load_sem, x_s, x_r, c_s, c_r, px_s, px_r, pz_s, pz_r, hz_s, hz_r, hx_s, hx_r, y_s, y_r, f_s, f_r, a_s, a_r,
):
    x = lax.axis_index("dom")
    tp = lax.axis_index("tp")
    z = lax.axis_index("dp")
    core = lax.rem(tp, 2)
    y = lax.rem(tp // 2, 8)
    h = tp // 16

    def plane(i, j):
        return (lax.rem(x + i, 4), tp, lax.rem(z + j, 4))

    def chip(i, j):
        return (x, lax.rem(h + i, 2) * 16 + lax.rem(y + j, 8) * 2 + core, z)

    sibling = (x, tp + 1 - 2 * core, z)

    def send(src, dst, ss, rs, to):
        cp = pltpu.make_async_remote_copy(
            src_ref=src, dst_ref=dst, send_sem=ss, recv_sem=rs, device_id=to, device_id_type=MESH
        )
        cp.start()
        return cp

    loads = [
        pltpu.make_async_copy(src, dst, load_sem.at[n])
        for n, (src, dst) in enumerate(
            [(q_hbm.at[0], q), (k_hbm.at[0], k), (v_hbm.at[0], v), (wg_hbm, wg), (wu_hbm, wu), (wd_hbm, wd)]
        )
    ]
    for cp in loads:
        cp.start()

    barrier = pltpu.get_barrier_semaphore()
    partners = [chip(i, j) for i, j in CHIPS] + [sibling] + [plane(i, j) for i, j in PLANE]
    for to in partners:
        pl.semaphore_signal(barrier, inc=1, device_id=to, device_id_type=MESH)
    xp[0, 0, 0] = fold(rows_ref[...].astype(F32)).astype(BF16)
    pl.semaphore_wait(barrier, len(partners))

    xs = [
        send(xp.at[0, 0, 0], xp.at[0, i, j], x_s.at[i, j], x_r.at[i, j], chip(i, j)) for i, j in CHIPS
    ]

    p = x * 4 + z
    sub, lane = iota((16, 16), 0), iota((16, 16), 1)
    counts = jnp.broadcast_to(count_ref[...].astype(F32), (16, 16))
    count_col = jnp.sum(jnp.where(lane == sub, counts, 0.0), axis=1, keepdims=True)
    start_lane = jnp.sum(jnp.where(sub < lane, count_col, 0.0), axis=0, keepdims=True)
    end_lane = jnp.sum(jnp.where(sub <= lane, count_col, 0.0), axis=0, keepdims=True)
    start_col = jnp.sum(jnp.where(lane < sub, counts, 0.0), axis=1, keepdims=True)
    end_col = start_col + count_col
    block = (p * 4 + (iota((8, 16), 0) & 3)).astype(F32)
    mine = jnp.logical_and(start_lane <= block, block < end_lane)
    trim_of = jnp.sum(jnp.where(mine, trim_ref[...].astype(F32), 0.0), axis=1, keepdims=True)
    end_of = jnp.sum(jnp.where(mine, end_lane, 0.0), axis=1, keepdims=True)
    limit = jnp.where(block[:, :1] == end_of - 1.0, 128.0 - trim_of, 128.0)
    pos = iota((8, 512), 1)
    live = jnp.logical_and(pos // 128 == (iota((8, 512), 0) & 3), (pos & 127).astype(F32) < limit)
    bias8 = jnp.where(live, 0.0, NEG)
    bias = jnp.concatenate([bias8] * 8, axis=0)
    onehot = jnp.where(mine, 1.0, 0.0).astype(BF16)
    is_slot = (iota((64, 128), 0) & 7) < 4
    stat_lane = iota((64, 128), 1)

    for cp in loads[:3]:
        cp.wait()
    for n in range(KEY_HEADS):
        chosen = jnp.dot(onehot, q[:, n * 1024 : (n + 1) * 1024], preferred_element_type=F32)
        query = jnp.concatenate([chosen[:, j * 128 : (j + 1) * 128] for j in range(8)], axis=0).astype(BF16)
        scores = lax.dot_general(
            query, k[:, n * 128 : (n + 1) * 128], (((1,), (1,)), ((), ())), preferred_element_type=F32
        ) * (HEAD_SIZE ** -0.5) + bias
        top = jnp.max(scores, axis=1, keepdims=True).astype(BF16).astype(F32)
        weights = jnp.exp(scores - top).astype(BF16)
        total = jnp.sum(weights.astype(F32), axis=1, keepdims=True)
        total_hi = total.astype(BF16).astype(F32)
        numer = jnp.dot(weights, v[:, n * 128 : (n + 1) * 128], preferred_element_type=F32)
        stat = jnp.where(stat_lane < 32, top, jnp.where(stat_lane < 64, total_hi, total - total_hi))
        tile = jnp.where(is_slot, numer, stat).astype(BF16)
        asend[2 * n] = tile[:32]
        asend[2 * n + 1] = tile[32:]
    sends_a = [
        send(
            asend.at[lax.rem(x + i, 4) * 4 + lax.rem(z + j, 4)], ar.at[i * 4 + j],
            a_s.at[i * 4 + j], a_r.at[i * 4 + j], plane(i, j),
        )
        for i, j in PLANE
    ]
    ar[0] = asend[p]

    for cp in xs:
        cp.wait()
    to_sibling = send(xp.at[0], xp.at[1], c_s, c_r, sibling)

    def place(c):
        for i in range(2):
            for j in range(0, 8, 2):
                a, b = xp[c, i, j].astype(F32), xp[c, i, j + 1].astype(F32)
                at = i * 128 + c * 64 + j * 8
                xmat[at : at + 16, :256] = jnp.concatenate([a[:8], b[:8]], axis=0).astype(BF16)
                xmat[at : at + 16, 256:] = jnp.concatenate([a[8:], b[8:]], axis=0).astype(BF16)

    place(0)
    to_sibling.wait()
    place(1)

    loads[3].wait()
    loads[4].wait()
    for w, base in ((wg, 0), (wu, 896)):
        for lo, hi in ((0, 256), (256, 512), (512, 768), (768, 896)):
            part = jnp.dot(xmat[...], w[:, lo:hi], preferred_element_type=F32)
            psend[:, :, :, base + lo : base + hi] = part.astype(BF16).reshape(4, 4, 16, hi - lo)

    sends_px = [
        send(psend.at[lax.rem(x + i, 4)], xr.at[i], px_s.at[i], px_r.at[i], plane(i, 0)) for i in (2, 1, 3)
    ]

    for cp in sends_a:
        cp.wait()
    col = iota((16, 128), 1)
    from_block = ((((x + 4 - col // 32) & 3) * 4 + ((z + 4 - (col // 8 & 3)) & 3)) * 4 + (col & 3)).astype(F32)
    owns = jnp.logical_and(jnp.logical_and(start_col <= from_block, from_block < end_col), (col & 7) >= 4)
    gathered = ar[...].astype(F32)
    for j in range(4):
        part = gathered[:, j * 8 : (j + 1) * 8, :].reshape(128, 128)
        turned = part.T
        tops, totals = turned[0:1], turned[32:33] + turned[64:65]
        top = jnp.max(jnp.where(owns, tops, NEG), axis=1, keepdims=True)
        scale = jnp.exp(jnp.where(owns, tops - top, NEG))
        den = jnp.sum(scale * totals, axis=1, keepdims=True)
        num = jnp.dot(
            pltpu.roll(scale, 124, 1), part, precision=lax.Precision.HIGHEST, preferred_element_type=F32
        )
        attn_ref[0, :, j * 128 : (j + 1) * 128] = (num / den).astype(BF16)

    for cp in sends_px:
        cp.wait()

    def across_x(at):
        total = psend[x, at].astype(F32)
        for i in (1, 2, 3):
            total = total + xr[i, at].astype(F32)
        return total

    sends_pz = []
    for j in (2, 1, 3):
        at = lax.rem(z + j, 4)
        zsend[j] = across_x(at).astype(BF16)
        sends_pz.append(send(zsend.at[j], zr.at[j], pz_s.at[j], pz_r.at[j], plane(0, j)))
    summed = across_x(z)
    for cp in sends_pz:
        cp.wait()
    for j in (1, 2, 3):
        summed = summed + zr[j].astype(F32)
    gate, up = summed[:, :896], summed[:, 896:]
    hall[x, z] = (gate / (1.0 + jnp.exp(-gate)) * up).astype(BF16)

    for cp in [
        send(hall.at[x, z], hall.at[x, z], hz_s.at[j], hz_r.at[j], plane(0, j)) for j in (2, 1, 3)
    ]:
        cp.wait_send()
    for j in (1, 2, 3):
        at = lax.rem(z + 4 - j, 4)
        pltpu.make_async_copy(hall.at[x, at], hall.at[x, at], hz_r.at[j]).wait()
    for cp in [send(hall.at[x], hall.at[x], hx_s.at[i], hx_r.at[i], plane(i, 0)) for i in (2, 1, 3)]:
        cp.wait_send()
    for i in (1, 2, 3):
        at = lax.rem(x + 4 - i, 4)
        pltpu.make_async_copy(hall.at[at], hall.at[at], hx_r.at[i]).wait()

    loads[5].wait()
    down = jnp.dot(hall[...].reshape(256, 896), wd[...], preferred_element_type=F32)
    for i in range(2):
        ysend[i] = down[i * 128 + 64 : i * 128 + 128].astype(BF16)
    to_sibling = send(ysend, yr, y_s, y_r, sibling)
    to_sibling.wait()
    sends_f = []
    for i, j in CHIPS + [(0, 0)]:
        at = i * 128 + j * 8
        rows = down[at : at + 8] + yr[i, j * 8 // 16 * 16 : j * 8 // 16 * 16 + 16].astype(F32)[j % 2 * 8 : j % 2 * 8 + 8]
        piece = fold(rows)
        if i or j:
            fsend[i, j] = piece.astype(BF16)
            sends_f.append(send(fsend.at[i, j], fr.at[i, j], f_s.at[i, j], f_r.at[i, j], chip(2 - i, 8 - j)))
    for cp in sends_f:
        cp.wait()
    for i, j in CHIPS:
        piece = piece + fr[i, j].astype(F32)
    ffn_ref[...] = unfold(piece).astype(BF16)


def shards(query, key_block_pool, value_block_pool, row_blocks, trim, ffn_in, w_gate, w_up, w_down):
    any_ = pl.BlockSpec(memory_space=pl.ANY)
    vmem = pl.BlockSpec(memory_space=pltpu.VMEM)
    dma = pltpu.SemaphoreType.DMA
    return pl.pallas_call(
        kernel,
        out_shape=(jax.ShapeDtypeStruct((1, 16, 512), BF16), jax.ShapeDtypeStruct((8, 512), BF16)),
        in_specs=[any_, any_, any_, vmem, vmem, vmem, any_, any_, any_],
        out_specs=(vmem, vmem),
        scratch_shapes=[
            pltpu.VMEM((16, 8192), BF16),
            pltpu.VMEM((512, 1024), BF16),
            pltpu.VMEM((512, 1024), BF16),
            pltpu.VMEM((512, 896), BF16),
            pltpu.VMEM((512, 896), BF16),
            pltpu.VMEM((896, 512), BF16),
            pltpu.VMEM((2, 2, 8, 16, 256), BF16),
            pltpu.VMEM((256, 512), BF16),
            pltpu.VMEM((4, 4, 16, 1792), BF16),
            pltpu.VMEM((4, 4, 16, 1792), BF16),
            pltpu.VMEM((4, 16, 1792), BF16),
            pltpu.VMEM((4, 16, 1792), BF16),
            pltpu.VMEM((4, 4, 16, 896), BF16),
            pltpu.VMEM((2, 64, 512), BF16),
            pltpu.VMEM((2, 64, 512), BF16),
            pltpu.VMEM((2, 8, 16, 256), BF16),
            pltpu.VMEM((2, 8, 16, 256), BF16),
            pltpu.VMEM((16, 32, 128), BF16),
            pltpu.VMEM((16, 32, 128), BF16),
            dma((6,)),
            dma((2, 8)), dma((2, 8)),
            dma, dma,
            dma((4,)), dma((4,)),
            dma((4,)), dma((4,)),
            dma((4,)), dma((4,)),
            dma((4,)), dma((4,)),
            dma, dma,
            dma((2, 8)), dma((2, 8)),
            dma((16,)), dma((16,)),
        ],
        compiler_params=pltpu.CompilerParams(
            collective_id=0, has_side_effects=True, vmem_limit_bytes=48 << 20
        ),
        name="decode_step",
    )(query, key_block_pool, value_block_pool, row_blocks, trim, ffn_in, w_gate, w_up, w_down)


def solution(mesh):
    in_specs = (
        P("tp", None, None),
        P("tp", ("dom", "dp"), None),
        P("tp", ("dom", "dp"), None),
        P("tp", None),
        P("tp", None),
        P("tp", ("dom", "dp")),
        P(("dom", "dp"), "tp"),
        P(("dom", "dp"), "tp"),
        P("tp", ("dom", "dp")),
    )
    out_specs = (P("tp", None, ("dom", "dp")), P("tp", ("dom", "dp")))
    return jax.shard_map(shards, mesh=mesh, in_specs=in_specs, out_specs=out_specs, check_vma=False)
```

time: 465 us -> 78.7 us (0.17)
  waiting for transfers between devices: 236 us -> 0 us
  blocking collectives: 195 us -> 0 us
  Pallas kernels: 0 us -> 67.5 us
  between operations: 14.6 us -> 0.66 us
  local copies, waits for them, and re-layouts: 2.68 us -> 10.1 us
  matrix products: 6.92 us -> 0 us
  other arithmetic: 5.14 us -> 0 us
    reduce_scatter x2 -> x0, waiting for transfers between devices: 147 us -> none  [the longest x1 131 us: ffn_part(): lax.psum_scatter(jnp.dot(hidden, w_down, preferred_element_type=jnp.float...]
    psum x1 -> x0, waiting for transfers between devices: 88.8 us -> none  [ffn_part(): summed = lax.psum(partial_sums, ('dom', 'dp'))]
    pmax x1 -> x0, blocking collectives: 68.5 us -> none  [attention_part(): top = lax.pmax(local_top, ('dom', 'dp'))]
    pallas_call x0 -> x1, Pallas kernels: none -> 67.5 us  [shards(): pl.pallas_call(kernel, out_shape=(jax.ShapeDtypeStruct((1, 16, 512), BF16...]
    unnamed x1 -> x0, blocking collectives: 66.1 us -> none
    all_gather x1 -> x0, blocking collectives: 60.9 us -> none  [ffn_part(): piece = lax.all_gather(ffn_in, 'tp', axis=0, tiled=True)]
    unnamed x20, local copies, waits for them, and re-layouts: 2.43 us -> 10.1 us
    dot_general x9 -> x0, matrix products: 6.92 us -> none  [the longest x1 2.76 us: ffn_part(): jnp.dot(hidden, w_down, preferred_element_type=jnp.float32)]
  transfers between devices with their start and end apart: 3 -> 0, of which waited for: 3 -> 0; matrix products, arithmetic and copies ran while one was open for 2% -> 0% of each run, Pallas kernels for 0% -> 0%
where the time goes in v1:
time: 78.7 us; the launch traced here: 78.3 us
  Pallas kernels  67.5 us (86%)
  local copies, waits for them, and re-layouts  10.1 us (13%)
    pallas_call x1, Pallas kernels, shards(): pl.pallas_call(kernel, out_shape=(jax.ShapeDtypeStruct((1, 16, 512), BF16...  67.5 us
    unnamed x20, local copies, waits for them, and re-layouts  10.1 us

profile of v1, /device:TPU:1, one launch (start us, length us, event | category | flops | bytes accessed | tf_op | source)
XLA Modules:
  0.0 78.3 jit_solution(7899486997761813844)
XLA Ops:
  0.6 0.0 copy-start
  0.6 1.2 %copy-done = bf16[1,512,1024]{2,1,0:T(8,128)(2,1)S(1)} copy-done((bf16[1,512,1024]{2,1,0:T(8,128)(2,1)S(1)}, bf16[1,512,1024]{2,1,0:T(8,128)(2,1)}, u32[]{:S(2)}) %copy-start) | copy-done | bytes 1048600
  1.9 0.0 copy-start.1
  1.9 1.2 %copy-done.1 = bf16[1,512,1024]{2,1,0:T(8,128)(2,1)S(1)} copy-done((bf16[1,512,1024]{2,1,0:T(8,128)(2,1)S(1)}, bf16[1,512,1024]{2,1,0:T(8,128)(2,1)}, u32[]{:S(2)}) %copy-start.1) | copy-done | bytes 1048600
  3.1 0.0 copy-start.2
  3.1 1.2 %copy-done.2 = bf16[512,896]{1,0:T(8,128)(2,1)S(1)} copy-done((bf16[512,896]{1,0:T(8,128)(2,1)S(1)}, bf16[512,896]{1,0:T(8,128)(2,1)}, u32[]{:S(2)}) %copy-start.2) | copy-done | bytes 917528
  4.3 0.0 copy-start.3
  4.3 1.2 %copy-done.3 = bf16[512,896]{1,0:T(8,128)(2,1)S(1)} copy-done((bf16[512,896]{1,0:T(8,128)(2,1)S(1)}, bf16[512,896]{1,0:T(8,128)(2,1)}, u32[]{:S(2)}) %copy-start.3) | copy-done | bytes 917528
  5.4 0.0 copy-start.4
  5.4 1.2 %copy-done.4 = bf16[896,512]{1,0:T(8,128)(2,1)S(1)} copy-done((bf16[896,512]{1,0:T(8,128)(2,1)S(1)}, bf16[896,512]{1,0:T(8,128)(2,1)}, u32[]{:S(2)}) %copy-start.4) | copy-done | bytes 917528
  6.6 0.0 copy-start.5
  6.6 0.9 %copy-done.5 = bf16[1,16,8192]{2,1,0:T(8,128)(2,1)S(1)} copy-done((bf16[1,16,8192]{2,1,0:T(8,128)(2,1)S(1)}, bf16[1,16,8192]{2,1,0:T(8,128)(2,1)}, u32[]{:S(2)}) %copy-start.5) | copy-done | bytes 262168
  7.6 0.0 copy-start.6
  7.6 0.7 copy-done.6
  8.3 0.0 copy-start.7
  8.3 0.7 copy-done.7
  8.9 0.0 copy-start.8
  8.9 0.7 copy-done.8
  9.6 67.5 %decode_step.1 = (bf16[1,16,512]{2,1,0:T(8,128)(2,1)S(1)}, bf16[8,512]{1,0:T(8,128)(2,1)S(1)}) custom-call(bf16[1,16,8192]{2,1,0:T(8,128)(2,1)S(1)} %copy-done.5, bf16[1,512,1024]{2,1,0:T(8,128)(2,1)S(1)} %copy-done, bf16[1,512,1024]{2,1,0:T(8,128)(2,1)S(1)} %copy-done.1, s32[1,16]{1,0:T(1,128)S(1)} %copy-done.7, s32[1,16]{1,0:T(1,128)S(1)} %copy-done.8, ...), custom_call_target="tpu_custom_call" | custom-call | tf_op jit(solution)/shard_map/decode_step/pallas_call | solution.py:233
  77.1 0.6 copy.13
  77.7 0.6 copy.14
Async XLA Ops:
  0.6 1.2 %copy-start = (bf16[1,512,1024]{2,1,0:T(8,128)(2,1)S(1)}, bf16[1,512,1024]{2,1,0:T(8,128)(2,1)}, u32[]{:S(2)}) copy-start(bf16[1,512,1024]{2,1,0:T(8,128)(2,1)} %k_hbm.1) | copy-start | bytes 3145732
  1.9 1.2 %copy-start.1 = (bf16[1,512,1024]{2,1,0:T(8,128)(2,1)S(1)}, bf16[1,512,1024]{2,1,0:T(8,128)(2,1)}, u32[]{:S(2)}) copy-start(bf16[1,512,1024]{2,1,0:T(8,128)(2,1)} %v_hbm.1) | copy-start | bytes 3145732
  3.1 1.2 %copy-start.2 = (bf16[512,896]{1,0:T(8,128)(2,1)S(1)}, bf16[512,896]{1,0:T(8,128)(2,1)}, u32[]{:S(2)}) copy-start(bf16[512,896]{1,0:T(8,128)(2,1)} %wg_hbm.1) | copy-start | bytes 2752516
  4.3 1.2 %copy-start.3 = (bf16[512,896]{1,0:T(8,128)(2,1)S(1)}, bf16[512,896]{1,0:T(8,128)(2,1)}, u32[]{:S(2)}) copy-start(bf16[512,896]{1,0:T(8,128)(2,1)} %wu_hbm.1) | copy-start | bytes 2752516
  5.4 1.2 %copy-start.4 = (bf16[896,512]{1,0:T(8,128)(2,1)S(1)}, bf16[896,512]{1,0:T(8,128)(2,1)}, u32[]{:S(2)}) copy-start(bf16[896,512]{1,0:T(8,128)(2,1)} %wd_hbm.1) | copy-start | bytes 2752516
  6.6 0.9 %copy-start.5 = (bf16[1,16,8192]{2,1,0:T(8,128)(2,1)S(1)}, bf16[1,16,8192]{2,1,0:T(8,128)(2,1)}, u32[]{:S(2)}) copy-start(bf16[1,16,8192]{2,1,0:T(8,128)(2,1)} %q_hbm.1) | copy-start | bytes 786436
  7.6 0.7 copy-start.6
  8.3 0.7 copy-start.7
  8.9 0.7 copy-start.8

commit v2 on v1

--- a/solution.py
+++ b/solution.py
@@ -15,6 +15,7 @@
 
 PLANE = [(i, j) for i in range(4) for j in range(4) if i or j]
 CHIPS = [(i, j) for i in range(2) for j in range(8) if i or j]
+PARTS = [(0, 0, 512), (1, 0, 512), (1, 512, 384), (0, 512, 384)]
 
 
 def iota(shape, axis):
@@ -33,9 +34,10 @@
     q_hbm, k_hbm, v_hbm, count_ref, trim_ref, rows_ref, wg_hbm, wu_hbm, wd_hbm,
     attn_ref, ffn_ref,
     q, k, v, wg, wu, wd,
-    xp, xmat, psend, xr, zsend, zr, hall, ysend, yr, fsend, fr, asend, ar,
+    xp, xmat, psend_0, psend_1, psend_2, psend_3, xr_0, xr_1, xr_2, xr_3, zsend, zr, hall, down, ysend, yr, fsend, fr, asend, ar,
     load_sem, x_s, x_r, c_s, c_r, px_s, px_r, pz_s, pz_r, hz_s, hz_r, hx_s, hx_r, y_s, y_r, f_s, f_r, a_s, a_r,
 ):
+    psend, xr = (psend_0, psend_1, psend_2, psend_3), (xr_0, xr_1, xr_2, xr_3)
     x = lax.axis_index("dom")
     tp = lax.axis_index("tp")
     z = lax.axis_index("dp")
@@ -58,6 +60,9 @@
         cp.start()
         return cp
 
+    def arrived(ref, sem):
+        pltpu.make_async_copy(ref, ref, sem).wait()
+
     loads = [
         pltpu.make_async_copy(src, dst, load_sem.at[n])
         for n, (src, dst) in enumerate(
@@ -74,9 +79,10 @@
     xp[0, 0, 0] = fold(rows_ref[...].astype(F32)).astype(BF16)
     pl.semaphore_wait(barrier, len(partners))
 
-    xs = [
-        send(xp.at[0, 0, 0], xp.at[0, i, j], x_s.at[i, j], x_r.at[i, j], chip(i, j)) for i, j in CHIPS
-    ]
+    xs = {
+        (i, j): send(xp.at[0, 0, 0], xp.at[i, 0, j], x_s.at[i, j], x_r.at[i, j], chip(i, j))
+        for i, j in CHIPS
+    }
 
     p = x * 4 + z
     sub, lane = iota((16, 16), 0), iota((16, 16), 1)
@@ -116,6 +122,141 @@
         tile = jnp.where(is_slot, numer, stat).astype(BF16)
         asend[2 * n] = tile[:32]
         asend[2 * n + 1] = tile[32:]
+    def gather(half):
+        for j in range(8):
+            if half or j:
+                xs[half, j].wait()
+        to_sibling = send(xp.at[half, 0], xp.at[half, 1], c_s.at[half], c_r.at[half], sibling)
+        for c in range(2):
+            if c:
+                to_sibling.wait()
+            for j in range(0, 8, 2):
+                a, b = xp[half, c, j].astype(F32), xp[half, c, j + 1].astype(F32)
+                at = half * 128 + c * 64 + j * 8
+                xmat[at : at + 16, :256] = jnp.concatenate([a[:8], b[:8]], axis=0).astype(BF16)
+                xmat[at : at + 16, 256:] = jnp.concatenate([a[8:], b[8:]], axis=0).astype(BF16)
+
+    def gate_up(n):
+        half, first, units = PARTS[n]
+        rows = xmat[half * 128 : half * 128 + 128, :]
+        for lo in range(0, units, 256):
+            wide = min(256, units - lo)
+            g = jnp.dot(rows, wg[:, first + lo : first + lo + wide], preferred_element_type=F32)
+            u = jnp.dot(rows, wu[:, first + lo : first + lo + wide], preferred_element_type=F32)
+            both = jnp.concatenate([g.reshape(16, 8, wide), u.reshape(16, 8, wide)], axis=1)
+            psend[n][:, :, :, lo : lo + wide] = both.astype(BF16).reshape(4, 4, 16, wide)
+        return [
+            send(psend[n].at[lax.rem(x + i, 4)], xr[n].at[i], px_s.at[n, i], px_r.at[n, i], plane(i, 0))
+            for i in (2, 1, 3)
+        ]
+
+    kept = {}
+
+    def over_x(n, copies):
+        units = PARTS[n][2]
+        for cp in copies:
+            cp.wait()
+
+        def total(at):
+            value = psend[n][x, at].astype(F32)
+            for i in (1, 2, 3):
+                value = value + xr[n][i, at].astype(F32)
+            return value
+
+        out = []
+        for j in (2, 1, 3):
+            zsend[n, j, :, :units] = total(lax.rem(z + j, 4)).astype(BF16)
+            out.append(
+                send(
+                    zsend.at[n, j, :, pl.ds(0, units)], zr.at[n, j, :, pl.ds(0, units)],
+                    pz_s.at[n, j], pz_r.at[n, j], plane(0, j),
+                )
+            )
+        kept[n] = total(z)
+        return out
+
+    def over_z(n, copies):
+        units = PARTS[n][2]
+        for cp in copies:
+            cp.wait()
+        value = kept[n]
+        for j in (1, 2, 3):
+            value = value + zr[n, j, :, :units].astype(F32)
+        gate, up = value[:8], value[8:]
+        hidden = gate / (1.0 + jnp.exp(-gate)) * up
+        if units < 512:
+            hidden = jnp.concatenate([hidden, jnp.zeros((8, 512 - units), F32)], axis=1)
+        hall[n, x, z] = fold(hidden).astype(BF16)
+        return [
+            send(hall.at[n, x, z], hall.at[n, x, z], hz_s.at[n, j], hz_r.at[n, j], plane(0, j))
+            for j in (2, 1, 3)
+        ]
+
+    def gather_z(n, copies):
+        for cp in copies:
+            cp.wait_send()
+        for j in (1, 2, 3):
+            arrived(hall.at[n, x, lax.rem(z + 4 - j, 4)], hz_r.at[n, j])
+        return [
+            send(hall.at[n, x], hall.at[n, x], hx_s.at[n, i], hx_r.at[n, i], plane(i, 0)) for i in (2, 1, 3)
+        ]
+
+    def gather_x(n, copies):
+        half, first, units = PARTS[n]
+        for cp in copies:
+            cp.wait_send()
+        for i in (1, 2, 3):
+            arrived(hall.at[n, lax.rem(x + 4 - i, 4)], hx_r.at[n, i])
+        rows = hall[n].astype(F32).reshape(16, 16, 256)
+        left = rows[:, :8].reshape(128, 256).astype(BF16)
+        right = rows[:, 8:].reshape(128, 256).astype(BF16)[:, : units - 256]
+        return jnp.dot(left, wd[first : first + 256, :], preferred_element_type=F32) + jnp.dot(
+            right, wd[first + 256 : first + units, :], preferred_element_type=F32
+        )
+
+    def other_core(half, rows):
+        down[half] = rows[:64]
+        ysend[half] = rows[64:].astype(BF16)
+        return send(ysend.at[half], yr.at[half], y_s.at[half], y_r.at[half], sibling)
+
+    def owners(half, copy):
+        copy.wait()
+        rows = down[half] + yr[half].astype(F32)
+        out = []
+        for j in range(8):
+            piece = fold(rows[j * 8 : j * 8 + 8])
+            if half == 0 and j == 0:
+                kept["own"] = piece
+                continue
+            fsend[half, j] = piece.astype(BF16)
+            out.append(
+                send(fsend.at[half, j], fr.at[half, j], f_s.at[half, j], f_r.at[half, j], chip(2 - half, 8 - j))
+            )
+        return out
+
+    gather(0)
+    loads[3].wait()
+    loads[4].wait()
+    px = {0: gate_up(0)}
+    gather(1)
+    px[1] = gate_up(1)
+    px[2] = gate_up(2)
+    px[3] = gate_up(3)
+    pz = {0: over_x(0, px[0])}
+    pz[1] = over_x(1, px[1])
+    hz = {0: over_z(0, pz[0])}
+    pz[2] = over_x(2, px[2])
+    hz[1] = over_z(1, pz[1])
+    hx = {0: gather_z(0, hz[0])}
+    pz[3] = over_x(3, px[3])
+    hz[2] = over_z(2, pz[2])
+    hx[1] = gather_z(1, hz[1])
+    hz[3] = over_z(3, pz[3])
+    hx[2] = gather_z(2, hz[2])
+    loads[5].wait()
+    rows_b = gather_x(1, hx[1])
+    rows_a = gather_x(0, hx[0])
+    hx[3] = gather_z(3, hz[3])
     sends_a = [
         send(
             asend.at[lax.rem(x + i, 4) * 4 + lax.rem(z + j, 4)], ar.at[i * 4 + j],
@@ -125,33 +266,10 @@
     ]
     ar[0] = asend[p]
 
-    for cp in xs:
-        cp.wait()
-    to_sibling = send(xp.at[0], xp.at[1], c_s, c_r, sibling)
-
-    def place(c):
-        for i in range(2):
-            for j in range(0, 8, 2):
-                a, b = xp[c, i, j].astype(F32), xp[c, i, j + 1].astype(F32)
-                at = i * 128 + c * 64 + j * 8
-                xmat[at : at + 16, :256] = jnp.concatenate([a[:8], b[:8]], axis=0).astype(BF16)
-                xmat[at : at + 16, 256:] = jnp.concatenate([a[8:], b[8:]], axis=0).astype(BF16)
-
-    place(0)
-    to_sibling.wait()
-    place(1)
-
-    loads[3].wait()
-    loads[4].wait()
-    for w, base in ((wg, 0), (wu, 896)):
-        for lo, hi in ((0, 256), (256, 512), (512, 768), (768, 896)):
-            part = jnp.dot(xmat[...], w[:, lo:hi], preferred_element_type=F32)
-            psend[:, :, :, base + lo : base + hi] = part.astype(BF16).reshape(4, 4, 16, hi - lo)
-
-    sends_px = [
-        send(psend.at[lax.rem(x + i, 4)], xr.at[i], px_s.at[i], px_r.at[i], plane(i, 0)) for i in (2, 1, 3)
-    ]
-
+    to_core = other_core(1, rows_b + gather_x(2, hx[2]))
+    sends_b = owners(1, to_core)
+    to_core = other_core(0, rows_a + gather_x(3, hx[3]))
+    sends_f = sends_b + owners(0, to_core)
     for cp in sends_a:
         cp.wait()
     col = iota((16, 128), 1)
@@ -170,57 +288,9 @@
         )
         attn_ref[0, :, j * 128 : (j + 1) * 128] = (num / den).astype(BF16)
 
-    for cp in sends_px:
-        cp.wait()
-
-    def across_x(at):
-        total = psend[x, at].astype(F32)
-        for i in (1, 2, 3):
-            total = total + xr[i, at].astype(F32)
-        return total
-
-    sends_pz = []
-    for j in (2, 1, 3):
-        at = lax.rem(z + j, 4)
-        zsend[j] = across_x(at).astype(BF16)
-        sends_pz.append(send(zsend.at[j], zr.at[j], pz_s.at[j], pz_r.at[j], plane(0, j)))
-    summed = across_x(z)
-    for cp in sends_pz:
-        cp.wait()
-    for j in (1, 2, 3):
-        summed = summed + zr[j].astype(F32)
-    gate, up = summed[:, :896], summed[:, 896:]
-    hall[x, z] = (gate / (1.0 + jnp.exp(-gate)) * up).astype(BF16)
-
-    for cp in [
-        send(hall.at[x, z], hall.at[x, z], hz_s.at[j], hz_r.at[j], plane(0, j)) for j in (2, 1, 3)
-    ]:
-        cp.wait_send()
-    for j in (1, 2, 3):
-        at = lax.rem(z + 4 - j, 4)
-        pltpu.make_async_copy(hall.at[x, at], hall.at[x, at], hz_r.at[j]).wait()
-    for cp in [send(hall.at[x], hall.at[x], hx_s.at[i], hx_r.at[i], plane(i, 0)) for i in (2, 1, 3)]:
-        cp.wait_send()
-    for i in (1, 2, 3):
-        at = lax.rem(x + 4 - i, 4)
-        pltpu.make_async_copy(hall.at[at], hall.at[at], hx_r.at[i]).wait()
-
-    loads[5].wait()
-    down = jnp.dot(hall[...].reshape(256, 896), wd[...], preferred_element_type=F32)
-    for i in range(2):
-        ysend[i] = down[i * 128 + 64 : i * 128 + 128].astype(BF16)
-    to_sibling = send(ysend, yr, y_s, y_r, sibling)
-    to_sibling.wait()
-    sends_f = []
-    for i, j in CHIPS + [(0, 0)]:
-        at = i * 128 + j * 8
-        rows = down[at : at + 8] + yr[i, j * 8 // 16 * 16 : j * 8 // 16 * 16 + 16].astype(F32)[j % 2 * 8 : j % 2 * 8 + 8]
-        piece = fold(rows)
-        if i or j:
-            fsend[i, j] = piece.astype(BF16)
-            sends_f.append(send(fsend.at[i, j], fr.at[i, j], f_s.at[i, j], f_r.at[i, j], chip(2 - i, 8 - j)))
     for cp in sends_f:
         cp.wait()
+    piece = kept["own"]
     for i, j in CHIPS:
         piece = piece + fr[i, j].astype(F32)
     ffn_ref[...] = unfold(piece).astype(BF16)
@@ -244,11 +314,12 @@
             pltpu.VMEM((896, 512), BF16),
             pltpu.VMEM((2, 2, 8, 16, 256), BF16),
             pltpu.VMEM((256, 512), BF16),
-            pltpu.VMEM((4, 4, 16, 1792), BF16),
-            pltpu.VMEM((4, 4, 16, 1792), BF16),
-            pltpu.VMEM((4, 16, 1792), BF16),
-            pltpu.VMEM((4, 16, 1792), BF16),
-            pltpu.VMEM((4, 4, 16, 896), BF16),
+            *[pltpu.VMEM((4, 4, 16, part[2]), BF16) for part in PARTS],
+            *[pltpu.VMEM((4, 4, 16, part[2]), BF16) for part in PARTS],
+            pltpu.VMEM((4, 4, 16, 512), BF16),
+            pltpu.VMEM((4, 4, 16, 512), BF16),
+            pltpu.VMEM((4, 4, 4, 16, 256), BF16),
+            pltpu.VMEM((2, 64, 512), F32),
             pltpu.VMEM((2, 64, 512), BF16),
             pltpu.VMEM((2, 64, 512), BF16),
             pltpu.VMEM((2, 8, 16, 256), BF16),
@@ -257,17 +328,17 @@
             pltpu.VMEM((16, 32, 128), BF16),
             dma((6,)),
             dma((2, 8)), dma((2, 8)),
-            dma, dma,
-            dma((4,)), dma((4,)),
-            dma((4,)), dma((4,)),
-            dma((4,)), dma((4,)),
-            dma((4,)), dma((4,)),
-            dma, dma,
+            dma((2,)), dma((2,)),
+            dma((4, 4)), dma((4, 4)),
+            dma((4, 4)), dma((4, 4)),
+            dma((4, 4)), dma((4, 4)),
+            dma((4, 4)), dma((4, 4)),
+            dma((2,)), dma((2,)),
             dma((2, 8)), dma((2, 8)),
             dma((16,)), dma((16,)),
         ],
         compiler_params=pltpu.CompilerParams(
-            collective_id=0, has_side_effects=True, vmem_limit_bytes=48 << 20
+            collective_id=0, has_side_effects=True, vmem_limit_bytes=60 << 20
         ),
         name="decode_step",
     )(query, key_block_pool, value_block_pool, row_blocks, trim, ffn_in, w_gate, w_up, w_down)

time: 78.7 us -> 60.9 us (0.77)
  Pallas kernels: 67.5 us -> 58.1 us
  local copies, waits for them, and re-layouts: 10.1 us -> 1.93 us
    pallas_call x1, Pallas kernels: 67.5 us -> 58.1 us  [shards(): pl.pallas_call(kernel, out_shape=(jax.ShapeDtypeStruct((1, 16, 512), BF16...]
    unnamed x20 -> x4, local copies, waits for them, and re-layouts: 10.1 us -> 1.93 us
where the time goes in v2:
time: 60.9 us; the launch traced here: 60.7 us
  Pallas kernels  58.1 us (95%)
  local copies, waits for them, and re-layouts  1.93 us (3%)
  between operations  0.65 us (1%)
    pallas_call x1, Pallas kernels, shards(): pl.pallas_call(kernel, out_shape=(jax.ShapeDtypeStruct((1, 16, 512), BF16...  58.1 us
    unnamed x4, local copies, waits for them, and re-layouts  1.93 us

profile of v2, /device:TPU:1, one launch (start us, length us, event | category | flops | bytes accessed | tf_op | source)
XLA Modules:
  0.0 60.7 jit_solution(9479827277094743926)
XLA Ops:
  0.6 58.1 %decode_step.1 = (bf16[1,16,512]{2,1,0:T(8,128)(2,1)}, bf16[8,512]{1,0:T(8,128)(2,1)}) custom-call(bf16[1,16,8192]{2,1,0:T(8,128)(2,1)} %q_hbm.1, bf16[1,512,1024]{2,1,0:T(8,128)(2,1)} %k_hbm.1, bf16[1,512,1024]{2,1,0:T(8,128)(2,1)} %v_hbm.1, s32[1,16]{1,0:T(1,128)} %count_ref.1, s32[1,16]{1,0:T(1,128)} %trim_ref.1, bf16[8,512]{1,0:T(8,128)(2,1)} %rows_ref.1, ...), custom_call_target="tpu_custom_call" | custom-call | tf_op jit(solution)/shard_map/decode_step/pallas_call | solution.py:303
  58.7 0.0 copy-start
  58.8 1.3 %copy.13 = bf16[1,16,512]{2,1,0:T(8,128)(2,1)} copy(bf16[1,16,512]{2,1,0:T(8,128)(2,1)} %get-tuple-element.4) | data formatting | bytes 32768
  60.1 0.0 copy-done
  60.1 0.6 copy.14
Async XLA Ops:
  58.7 1.3 %copy-start = (bf16[8,512]{1,0:T(8,128)(2,1)S(1)}, bf16[8,512]{1,0:T(8,128)(2,1)}, u32[]{:S(2)}) copy-start(bf16[8,512]{1,0:T(8,128)(2,1)} %get-tuple-element.5) | copy-start | bytes 24580

commit v3 on v2

--- a/solution.py
+++ b/solution.py
@@ -15,7 +15,9 @@
 
 PLANE = [(i, j) for i in range(4) for j in range(4) if i or j]
 CHIPS = [(i, j) for i in range(2) for j in range(8) if i or j]
-PARTS = [(0, 0, 512), (1, 0, 512), (1, 512, 384), (0, 512, 384)]
+
+FAR_FIRST = sorted(PLANE, key=lambda t: -(min(t[0], 4 - t[0]) + min(t[1], 4 - t[1])))
+DIRECT = (3,)
 
 
 def iota(shape, axis):
@@ -34,10 +36,9 @@
     q_hbm, k_hbm, v_hbm, count_ref, trim_ref, rows_ref, wg_hbm, wu_hbm, wd_hbm,
     attn_ref, ffn_ref,
     q, k, v, wg, wu, wd,
-    xp, xmat, psend_0, psend_1, psend_2, psend_3, xr_0, xr_1, xr_2, xr_3, zsend, zr, hall, down, ysend, yr, fsend, fr, asend, ar,
-    load_sem, x_s, x_r, c_s, c_r, px_s, px_r, pz_s, pz_r, hz_s, hz_r, hx_s, hx_r, y_s, y_r, f_s, f_r, a_s, a_r,
+    xp, xmat, psend, xr, ztotal, zsend, zr, hall, down, ysend, yr, fsend, fr, asend, ar,
+    load_sem, x_s, x_r, c_s, c_r, px_s, px_r, pz_s, pz_r, hz_s, hz_r, hx_s, hx_r, hd_s, hd_r, y_s, y_r, f_s, f_r, a_s, a_r,
 ):
-    psend, xr = (psend_0, psend_1, psend_2, psend_3), (xr_0, xr_1, xr_2, xr_3)
     x = lax.axis_index("dom")
     tp = lax.axis_index("tp")
     z = lax.axis_index("dp")
@@ -63,6 +64,13 @@
     def arrived(ref, sem):
         pltpu.make_async_copy(ref, ref, sem).wait()
 
+    barrier = pltpu.get_barrier_semaphore()
+    partners = (
+        [chip(0, j) for j in range(1, 8)] + [chip(1, 0), sibling]
+        + [plane(i, 0) for i in (1, 2, 3)] + [plane(0, j) for j in (1, 2, 3)]
+    )
+    for to in partners:
+        pl.semaphore_signal(barrier, inc=1, device_id=to, device_id_type=MESH)
     loads = [
         pltpu.make_async_copy(src, dst, load_sem.at[n])
         for n, (src, dst) in enumerate(
@@ -71,18 +79,7 @@
     ]
     for cp in loads:
         cp.start()
-
-    barrier = pltpu.get_barrier_semaphore()
-    partners = [chip(i, j) for i, j in CHIPS] + [sibling] + [plane(i, j) for i, j in PLANE]
-    for to in partners:
-        pl.semaphore_signal(barrier, inc=1, device_id=to, device_id_type=MESH)
     xp[0, 0, 0] = fold(rows_ref[...].astype(F32)).astype(BF16)
-    pl.semaphore_wait(barrier, len(partners))
-
-    xs = {
-        (i, j): send(xp.at[0, 0, 0], xp.at[i, 0, j], x_s.at[i, j], x_r.at[i, j], chip(i, j))
-        for i, j in CHIPS
-    }
 
     p = x * 4 + z
     sub, lane = iota((16, 16), 0), iota((16, 16), 1)
@@ -107,92 +104,93 @@
 
     for cp in loads[:3]:
         cp.wait()
-    for n in range(KEY_HEADS):
-        chosen = jnp.dot(onehot, q[:, n * 1024 : (n + 1) * 1024], preferred_element_type=F32)
-        query = jnp.concatenate([chosen[:, j * 128 : (j + 1) * 128] for j in range(8)], axis=0).astype(BF16)
-        scores = lax.dot_general(
-            query, k[:, n * 128 : (n + 1) * 128], (((1,), (1,)), ((), ())), preferred_element_type=F32
-        ) * (HEAD_SIZE ** -0.5) + bias
-        top = jnp.max(scores, axis=1, keepdims=True).astype(BF16).astype(F32)
-        weights = jnp.exp(scores - top).astype(BF16)
-        total = jnp.sum(weights.astype(F32), axis=1, keepdims=True)
-        total_hi = total.astype(BF16).astype(F32)
-        numer = jnp.dot(weights, v[:, n * 128 : (n + 1) * 128], preferred_element_type=F32)
-        stat = jnp.where(stat_lane < 32, top, jnp.where(stat_lane < 64, total_hi, total - total_hi))
-        tile = jnp.where(is_slot, numer, stat).astype(BF16)
-        asend[2 * n] = tile[:32]
-        asend[2 * n + 1] = tile[32:]
-    def gather(half):
-        for j in range(8):
-            if half or j:
-                xs[half, j].wait()
-        to_sibling = send(xp.at[half, 0], xp.at[half, 1], c_s.at[half], c_r.at[half], sibling)
-        for c in range(2):
-            if c:
-                to_sibling.wait()
-            for j in range(0, 8, 2):
-                a, b = xp[half, c, j].astype(F32), xp[half, c, j + 1].astype(F32)
-                at = half * 128 + c * 64 + j * 8
-                xmat[at : at + 16, :256] = jnp.concatenate([a[:8], b[:8]], axis=0).astype(BF16)
-                xmat[at : at + 16, 256:] = jnp.concatenate([a[8:], b[8:]], axis=0).astype(BF16)
+    def attend(first, last):
+        for n in range(first, last):
+            chosen = jnp.dot(onehot, q[:, n * 1024 : (n + 1) * 1024], preferred_element_type=F32)
+            query = jnp.concatenate([chosen[:, j * 128 : (j + 1) * 128] for j in range(8)], axis=0).astype(BF16)
+            scores = lax.dot_general(
+                query, k[:, n * 128 : (n + 1) * 128], (((1,), (1,)), ((), ())), preferred_element_type=F32
+            ) * (HEAD_SIZE ** -0.5) + bias
+            top = jnp.max(scores, axis=1, keepdims=True).astype(BF16).astype(F32)
+            weights = jnp.exp(scores - top).astype(BF16)
+            total = jnp.sum(weights.astype(F32), axis=1, keepdims=True)
+            total_hi = total.astype(BF16).astype(F32)
+            numer = jnp.dot(weights, v[:, n * 128 : (n + 1) * 128], preferred_element_type=F32)
+            stat = jnp.where(stat_lane < 32, top, jnp.where(stat_lane < 64, total_hi, total - total_hi))
+            tile = jnp.where(is_slot, numer, stat).astype(BF16)
+            asend[2 * n] = tile[:32]
+            asend[2 * n + 1] = tile[32:]
+
+    attend(0, 0)
+    pl.semaphore_wait(barrier, len(partners))
+
+    xs = {}
+    xs[1, 0] = send(xp.at[0, 0, 0], xp.at[1, 0, 0], x_s.at[1, 0], x_r.at[1, 0], chip(1, 0))
+    for j in (4, 3, 5, 2, 6, 1, 7):
+        xs[0, j] = send(xp.at[0, 0, 0], xp.at[0, 0, j], x_s.at[0, j], x_r.at[0, j], chip(0, j))
+
+    attend(0, KEY_HEADS)
+
+    def put(half, c):
+        for j in range(0, 8, 2):
+            a, b = xp[half, c, j].astype(F32), xp[half, c, j + 1].astype(F32)
+            xmat[2 * half + c, j * 8 : j * 8 + 16, :256] = jnp.concatenate([a[:8], b[:8]], axis=0).astype(BF16)
+            xmat[2 * half + c, j * 8 : j * 8 + 16, 256:] = jnp.concatenate([a[8:], b[8:]], axis=0).astype(BF16)
+
+    def to_other_core(half):
+        return send(xp.at[half, 0], xp.at[half, 1], c_s.at[half], c_r.at[half], sibling)
 
     def gate_up(n):
-        half, first, units = PARTS[n]
-        rows = xmat[half * 128 : half * 128 + 128, :]
-        for lo in range(0, units, 256):
-            wide = min(256, units - lo)
-            g = jnp.dot(rows, wg[:, first + lo : first + lo + wide], preferred_element_type=F32)
-            u = jnp.dot(rows, wu[:, first + lo : first + lo + wide], preferred_element_type=F32)
-            both = jnp.concatenate([g.reshape(16, 8, wide), u.reshape(16, 8, wide)], axis=1)
-            psend[n][:, :, :, lo : lo + wide] = both.astype(BF16).reshape(4, 4, 16, wide)
+        rows = xmat[n]
+        for lo, hi in ((0, 256), (256, 512), (512, 768), (768, 896)):
+            g = jnp.dot(rows, wg[:, lo:hi], preferred_element_type=F32)
+            u = jnp.dot(rows, wu[:, lo:hi], preferred_element_type=F32)
+            both = jnp.concatenate([g.reshape(8, 8, hi - lo), u.reshape(8, 8, hi - lo)], axis=1)
+            psend[n, :, :, :, lo:hi] = both.astype(BF16).reshape(4, 2, 16, hi - lo)
         return [
-            send(psend[n].at[lax.rem(x + i, 4)], xr[n].at[i], px_s.at[n, i], px_r.at[n, i], plane(i, 0))
+            send(psend.at[n, lax.rem(x + i, 4)], xr.at[n, i], px_s.at[n, i], px_r.at[n, i], plane(i, 0))
             for i in (2, 1, 3)
         ]
 
-    kept = {}
-
     def over_x(n, copies):
-        units = PARTS[n][2]
         for cp in copies:
             cp.wait()
-
-        def total(at):
-            value = psend[n][x, at].astype(F32)
+        for r in range(2):
+            value = psend[n, x, r].astype(F32)
             for i in (1, 2, 3):
-                value = value + xr[n][i, at].astype(F32)
-            return value
-
-        out = []
-        for j in (2, 1, 3):
-            zsend[n, j, :, :units] = total(lax.rem(z + j, 4)).astype(BF16)
-            out.append(
-                send(
-                    zsend.at[n, j, :, pl.ds(0, units)], zr.at[n, j, :, pl.ds(0, units)],
-                    pz_s.at[n, j], pz_r.at[n, j], plane(0, j),
-                )
-            )
-        kept[n] = total(z)
-        return out
+                value = value + xr[n, i, r].astype(F32)
+            ztotal[n, 2 * r] = value[:, :512]
+            ztotal[n, 2 * r + 1, :, :384] = value[:, 512:]
+            ztotal[n, 2 * r + 1, :, 384:] = jnp.zeros((16, 128), F32)
+            zsend[n, 2 * r] = value[:, :512].astype(BF16)
+            zsend[n, 2 * r + 1, :, :384] = value[:, 512:].astype(BF16)
+            zsend[n, 2 * r + 1, :, 384:] = jnp.zeros((16, 128), BF16)
+        return [
+            send(zsend.at[n, lax.rem(z + j, 4)], zr.at[n, j], pz_s.at[n, j], pz_r.at[n, j], plane(0, j))
+            for j in (2, 1, 3)
+        ]
 
     def over_z(n, copies):
-        units = PARTS[n][2]
         for cp in copies:
             cp.wait()
-        value = kept[n]
+        value = ztotal[n, z]
         for j in (1, 2, 3):
-            value = value + zr[n, j, :, :units].astype(F32)
+            value = value + zr[n, j].astype(F32)
         gate, up = value[:8], value[8:]
-        hidden = gate / (1.0 + jnp.exp(-gate)) * up
-        if units < 512:
-            hidden = jnp.concatenate([hidden, jnp.zeros((8, 512 - units), F32)], axis=1)
-        hall[n, x, z] = fold(hidden).astype(BF16)
+        hall[n, x, z] = fold(gate / (1.0 + jnp.exp(-gate)) * up).astype(BF16)
+        if n in DIRECT:
+            return [
+                send(hall.at[n, x, z], hall.at[n, x, z], hd_s.at[n, i * 4 + j], hd_r.at[n, i * 4 + j], plane(i, j))
+                for i, j in FAR_FIRST
+            ]
         return [
             send(hall.at[n, x, z], hall.at[n, x, z], hz_s.at[n, j], hz_r.at[n, j], plane(0, j))
             for j in (2, 1, 3)
         ]
 
     def gather_z(n, copies):
+        if n in DIRECT:
+            return copies
         for cp in copies:
             cp.wait_send()
         for j in (1, 2, 3):
@@ -202,22 +200,26 @@
         ]
 
     def gather_x(n, copies):
-        half, first, units = PARTS[n]
         for cp in copies:
             cp.wait_send()
-        for i in (1, 2, 3):
-            arrived(hall.at[n, lax.rem(x + 4 - i, 4)], hx_r.at[n, i])
-        rows = hall[n].astype(F32).reshape(16, 16, 256)
-        left = rows[:, :8].reshape(128, 256).astype(BF16)
-        right = rows[:, 8:].reshape(128, 256).astype(BF16)[:, : units - 256]
-        return jnp.dot(left, wd[first : first + 256, :], preferred_element_type=F32) + jnp.dot(
-            right, wd[first + 256 : first + units, :], preferred_element_type=F32
-        )
+        if n in DIRECT:
+            for i, j in FAR_FIRST:
+                arrived(hall.at[n, lax.rem(x + 4 - i, 4), lax.rem(z + 4 - j, 4)], hd_r.at[n, i * 4 + j])
+        else:
+            for i in (1, 2, 3):
+                arrived(hall.at[n, lax.rem(x + 4 - i, 4)], hx_r.at[n, i])
+        rows = hall[n].astype(F32).reshape(8, 2, 2, 8, 256)
+        out = 0.0
+        for i, lo, hi in ((0, 0, 256), (1, 256, 512), (2, 512, 768), (3, 768, 896)):
+            part = rows[:, i // 2, i % 2].reshape(64, 256).astype(BF16)[:, : hi - lo]
+            out = out + jnp.dot(part, wd[lo:hi, :], preferred_element_type=F32)
+        return out
 
     def other_core(half, rows):
-        down[half] = rows[:64]
-        ysend[half] = rows[64:].astype(BF16)
+        ysend[half] = rows.astype(BF16)
         return send(ysend.at[half], yr.at[half], y_s.at[half], y_r.at[half], sibling)
+
+    kept = {}
 
     def owners(half, copy):
         copy.wait()
@@ -234,13 +236,26 @@
             )
         return out
 
-    gather(0)
+    xs[1, 0].wait()
+    for j in (4, 3, 5, 2, 6, 1, 7):
+        xs[1, j] = send(xp.at[1, 0, 0], xp.at[1, 0, j], x_s.at[1, j], x_r.at[1, j], chip(0, j))
+    for j in range(1, 8):
+        xs[0, j].wait()
+    cores_a = to_other_core(0)
+    put(0, 0)
     loads[3].wait()
     loads[4].wait()
     px = {0: gate_up(0)}
-    gather(1)
+    cores_a.wait()
+    put(0, 1)
     px[1] = gate_up(1)
+    for j in range(1, 8):
+        xs[1, j].wait()
+    cores_b = to_other_core(1)
+    put(1, 0)
     px[2] = gate_up(2)
+    cores_b.wait()
+    put(1, 1)
     px[3] = gate_up(3)
     pz = {0: over_x(0, px[0])}
     pz[1] = over_x(1, px[1])
@@ -254,9 +269,12 @@
     hz[3] = over_z(3, pz[3])
     hx[2] = gather_z(2, hz[2])
     loads[5].wait()
-    rows_b = gather_x(1, hx[1])
-    rows_a = gather_x(0, hx[0])
+    down[0] = gather_x(0, hx[0])
+    core_a = other_core(0, gather_x(1, hx[1]))
     hx[3] = gather_z(3, hz[3])
+    sends_f = owners(0, core_a)
+    down[1] = gather_x(2, hx[2])
+    core_b = other_core(1, gather_x(3, hx[3]))
     sends_a = [
         send(
             asend.at[lax.rem(x + i, 4) * 4 + lax.rem(z + j, 4)], ar.at[i * 4 + j],
@@ -266,10 +284,7 @@
     ]
     ar[0] = asend[p]
 
-    to_core = other_core(1, rows_b + gather_x(2, hx[2]))
-    sends_b = owners(1, to_core)
-    to_core = other_core(0, rows_a + gather_x(3, hx[3]))
-    sends_f = sends_b + owners(0, to_core)
+    sends_f = sends_f + owners(1, core_b)
     for cp in sends_a:
         cp.wait()
     col = iota((16, 128), 1)
@@ -302,7 +317,7 @@
     dma = pltpu.SemaphoreType.DMA
     return pl.pallas_call(
         kernel,
-        out_shape=(jax.ShapeDtypeStruct((1, 16, 512), BF16), jax.ShapeDtypeStruct((8, 512), BF16)),
+        out_shape=(pltpu.VMEM((1, 16, 512), BF16), pltpu.VMEM((8, 512), BF16)),
         in_specs=[any_, any_, any_, vmem, vmem, vmem, any_, any_, any_],
         out_specs=(vmem, vmem),
         scratch_shapes=[
@@ -313,9 +328,10 @@
             pltpu.VMEM((512, 896), BF16),
             pltpu.VMEM((896, 512), BF16),
             pltpu.VMEM((2, 2, 8, 16, 256), BF16),
-            pltpu.VMEM((256, 512), BF16),
-            *[pltpu.VMEM((4, 4, 16, part[2]), BF16) for part in PARTS],
-            *[pltpu.VMEM((4, 4, 16, part[2]), BF16) for part in PARTS],
+            pltpu.VMEM((4, 64, 512), BF16),
+            pltpu.VMEM((4, 4, 2, 16, 896), BF16),
+            pltpu.VMEM((4, 4, 2, 16, 896), BF16),
+            pltpu.VMEM((4, 4, 16, 512), F32),
             pltpu.VMEM((4, 4, 16, 512), BF16),
             pltpu.VMEM((4, 4, 16, 512), BF16),
             pltpu.VMEM((4, 4, 4, 16, 256), BF16),
@@ -333,6 +349,7 @@
             dma((4, 4)), dma((4, 4)),
             dma((4, 4)), dma((4, 4)),
             dma((4, 4)), dma((4, 4)),
+            dma((4, 16)), dma((4, 16)),
             dma((2,)), dma((2,)),
             dma((2, 8)), dma((2, 8)),
             dma((16,)), dma((16,)),

time: 60.9 us -> 56.9 us (0.934)
  Pallas kernels: 58.1 us -> 54.9 us
  local copies, waits for them, and re-layouts: 1.93 us -> 1.21 us
    pallas_call x1, Pallas kernels: 58.1 us -> 54.9 us  [shards(): pl.pallas_call(kernel, out_shape=(pltpu.VMEM((1, 16, 512), BF16), pltpu.V...]
    unnamed x4 -> x2, local copies, waits for them, and re-layouts: 1.93 us -> 1.21 us
where the time goes in v3:
time: 56.9 us; the launch traced here: 56.7 us
  Pallas kernels  54.9 us (96%)
  local copies, waits for them, and re-layouts  1.21 us (2%)
  between operations  0.64 us (1%)
    pallas_call x1, Pallas kernels, shards(): pl.pallas_call(kernel, out_shape=(pltpu.VMEM((1, 16, 512), BF16), pltpu.V...  54.9 us
    unnamed x2, local copies, waits for them, and re-layouts  1.21 us

profile of v3, /device:TPU:1, one launch (start us, length us, event | category | flops | bytes accessed | tf_op | source)
XLA Modules:
  0.0 56.7 jit_solution(14927580242063218222)
XLA Ops:
  0.6 54.9 %decode_step.1 = (bf16[1,16,512]{2,1,0:T(8,128)(2,1)S(1)}, bf16[8,512]{1,0:T(8,128)(2,1)S(1)}) custom-call(bf16[1,16,8192]{2,1,0:T(8,128)(2,1)} %q_hbm.1, bf16[1,512,1024]{2,1,0:T(8,128)(2,1)} %k_hbm.1, bf16[1,512,1024]{2,1,0:T(8,128)(2,1)} %v_hbm.1, s32[1,16]{1,0:T(1,128)} %count_ref.1, s32[1,16]{1,0:T(1,128)} %trim_ref.1, bf16[8,512]{1,0:T(8,128)(2,1)} %rows_ref.1, ...), custom_call_target="tpu_custom_call" | custom-call | tf_op jit(solution)/shard_map/decode_step/pallas_call | solution.py:318
  55.5 0.6 %copy.13 = bf16[1,16,512]{2,1,0:T(8,128)(2,1)} copy(bf16[1,16,512]{2,1,0:T(8,128)(2,1)S(1)} %get-tuple-element.2) | data formatting | bytes 32768
  56.1 0.6 %copy.14 = bf16[8,512]{1,0:T(8,128)(2,1)} copy(bf16[8,512]{1,0:T(8,128)(2,1)S(1)} %get-tuple-element.3) | data formatting | bytes 16384

commit v4 on v3

--- a/solution.py
+++ b/solution.py
@@ -17,7 +17,14 @@
 CHIPS = [(i, j) for i in range(2) for j in range(8) if i or j]
 
 FAR_FIRST = sorted(PLANE, key=lambda t: -(min(t[0], 4 - t[0]) + min(t[1], 4 - t[1])))
-DIRECT = (3,)
+DIRECT = (2, 3,)
+FAR, NEAR = (4, 3, 5, 2), (6, 1, 7, 0)
+PARTS = (
+    (0, [(0, j) for j in range(8)]),
+    (0, [(1, j) for j in range(8)]),
+    (1, [(c, j) for c in (0, 1) for j in FAR]),
+    (1, [(c, j) for c in (0, 1) for j in NEAR]),
+)
 
 
 def iota(shape, axis):
@@ -36,7 +43,7 @@
     q_hbm, k_hbm, v_hbm, count_ref, trim_ref, rows_ref, wg_hbm, wu_hbm, wd_hbm,
     attn_ref, ffn_ref,
     q, k, v, wg, wu, wd,
-    xp, xmat, psend, xr, ztotal, zsend, zr, hall, down, ysend, yr, fsend, fr, asend, ar,
+    xp, xmat, psend, xr, ztotal, zsend, zr, hall, down, ysend, yr, fsend, fr, asend, ax, ar,
     load_sem, x_s, x_r, c_s, c_r, px_s, px_r, pz_s, pz_r, hz_s, hz_r, hx_s, hx_r, hd_s, hd_r, y_s, y_r, f_s, f_r, a_s, a_r,
 ):
     x = lax.axis_index("dom")
@@ -118,10 +125,10 @@
             numer = jnp.dot(weights, v[:, n * 128 : (n + 1) * 128], preferred_element_type=F32)
             stat = jnp.where(stat_lane < 32, top, jnp.where(stat_lane < 64, total_hi, total - total_hi))
             tile = jnp.where(is_slot, numer, stat).astype(BF16)
-            asend[2 * n] = tile[:32]
-            asend[2 * n + 1] = tile[32:]
-
-    attend(0, 0)
+            asend[n // 2, n % 2 * 2] = tile[:32]
+            asend[n // 2, n % 2 * 2 + 1] = tile[32:]
+
+    attend(0, 2)
     pl.semaphore_wait(barrier, len(partners))
 
     xs = {}
@@ -129,13 +136,14 @@
     for j in (4, 3, 5, 2, 6, 1, 7):
         xs[0, j] = send(xp.at[0, 0, 0], xp.at[0, 0, j], x_s.at[0, j], x_r.at[0, j], chip(0, j))
 
-    attend(0, KEY_HEADS)
-
-    def put(half, c):
-        for j in range(0, 8, 2):
-            a, b = xp[half, c, j].astype(F32), xp[half, c, j + 1].astype(F32)
-            xmat[2 * half + c, j * 8 : j * 8 + 16, :256] = jnp.concatenate([a[:8], b[:8]], axis=0).astype(BF16)
-            xmat[2 * half + c, j * 8 : j * 8 + 16, 256:] = jnp.concatenate([a[8:], b[8:]], axis=0).astype(BF16)
+    attend(2, 8)
+
+    def put(n, first, last):
+        half, pieces = PARTS[n]
+        for e in range(first, last, 2):
+            a, b = xp[(half, *pieces[e])].astype(F32), xp[(half, *pieces[e + 1])].astype(F32)
+            xmat[n, e * 8 : e * 8 + 16, :256] = jnp.concatenate([a[:8], b[:8]], axis=0).astype(BF16)
+            xmat[n, e * 8 : e * 8 + 16, 256:] = jnp.concatenate([a[8:], b[8:]], axis=0).astype(BF16)
 
     def to_other_core(half):
         return send(xp.at[half, 0], xp.at[half, 1], c_s.at[half], c_r.at[half], sibling)
@@ -215,18 +223,19 @@
             out = out + jnp.dot(part, wd[lo:hi, :], preferred_element_type=F32)
         return out
 
-    def other_core(half, rows):
-        ysend[half] = rows.astype(BF16)
-        return send(ysend.at[half], yr.at[half], y_s.at[half], y_r.at[half], sibling)
+    def other_core(at, rows):
+        refs = [r.at[at // 2, pl.ds(at % 2 * 32, rows.shape[0])] for r in (ysend, yr)]
+        refs[0][...] = rows.astype(BF16)
+        return send(*refs, y_s.at[at], y_r.at[at], sibling)
 
     kept = {}
 
-    def owners(half, copy):
+    def owners(half, at, rows, order, copy):
         copy.wait()
-        rows = down[half] + yr[half].astype(F32)
+        rows = rows + yr[half, at : at + rows.shape[0]].astype(F32)
         out = []
-        for j in range(8):
-            piece = fold(rows[j * 8 : j * 8 + 8])
+        for t, j in order:
+            piece = fold(rows[t * 8 : t * 8 + 8])
             if half == 0 and j == 0:
                 kept["own"] = piece
                 continue
@@ -236,26 +245,40 @@
             )
         return out
 
+
+    sends_ax = [
+        send(asend.at[lax.rem(x + i, 4)], ax.at[i], a_s.at[i], a_r.at[i], plane(i, 0)) for i in (2, 1, 3)
+    ]
+    ax[0] = asend[x]
     xs[1, 0].wait()
     for j in (4, 3, 5, 2, 6, 1, 7):
         xs[1, j] = send(xp.at[1, 0, 0], xp.at[1, 0, j], x_s.at[1, j], x_r.at[1, j], chip(0, j))
     for j in range(1, 8):
         xs[0, j].wait()
     cores_a = to_other_core(0)
-    put(0, 0)
+    put(0, 0, 8)
     loads[3].wait()
     loads[4].wait()
     px = {0: gate_up(0)}
     cores_a.wait()
-    put(0, 1)
+    put(1, 0, 8)
     px[1] = gate_up(1)
+    for cp in sends_ax:
+        cp.wait()
+    sends_az = [
+        send(ax.at[:, lax.rem(z + j, 4)], ar.at[:, j], a_s.at[4 + j], a_r.at[4 + j], plane(0, j))
+        for j in (2, 1, 3)
+    ]
+    ar[:, 0] = ax[:, z]
     for j in range(1, 8):
         xs[1, j].wait()
     cores_b = to_other_core(1)
-    put(1, 0)
+    put(2, 0, 4)
+    put(3, 0, 4)
+    cores_b.wait()
+    put(2, 4, 8)
     px[2] = gate_up(2)
-    cores_b.wait()
-    put(1, 1)
+    put(3, 4, 8)
     px[3] = gate_up(3)
     pz = {0: over_x(0, px[0])}
     pz[1] = over_x(1, px[1])
@@ -269,28 +292,22 @@
     hz[3] = over_z(3, pz[3])
     hx[2] = gather_z(2, hz[2])
     loads[5].wait()
-    down[0] = gather_x(0, hx[0])
+    down[...] = gather_x(0, hx[0])
     core_a = other_core(0, gather_x(1, hx[1]))
     hx[3] = gather_z(3, hz[3])
-    sends_f = owners(0, core_a)
-    down[1] = gather_x(2, hx[2])
-    core_b = other_core(1, gather_x(3, hx[3]))
-    sends_a = [
-        send(
-            asend.at[lax.rem(x + i, 4) * 4 + lax.rem(z + j, 4)], ar.at[i * 4 + j],
-            a_s.at[i * 4 + j], a_r.at[i * 4 + j], plane(i, j),
-        )
-        for i, j in PLANE
-    ]
-    ar[0] = asend[p]
-
-    sends_f = sends_f + owners(1, core_b)
-    for cp in sends_a:
+    sends_f = owners(0, 0, down[...], [(j, j) for j in (4, 3, 5, 2, 6, 1, 7, 0)], core_a)
+    rows_far = gather_x(2, hx[2])
+    core_far = other_core(2, rows_far[32:])
+    sends_f = sends_f + owners(1, 0, rows_far[:32], list(enumerate(FAR)), core_far)
+    rows_near = gather_x(3, hx[3])
+    core_near = other_core(3, rows_near[32:])
+    sends_f = sends_f + owners(1, 32, rows_near[:32], list(enumerate(NEAR)), core_near)
+    for cp in sends_az:
         cp.wait()
     col = iota((16, 128), 1)
     from_block = ((((x + 4 - col // 32) & 3) * 4 + ((z + 4 - (col // 8 & 3)) & 3)) * 4 + (col & 3)).astype(F32)
     owns = jnp.logical_and(jnp.logical_and(start_col <= from_block, from_block < end_col), (col & 7) >= 4)
-    gathered = ar[...].astype(F32)
+    gathered = ar[...].astype(F32).reshape(16, 32, 128)
     for j in range(4):
         part = gathered[:, j * 8 : (j + 1) * 8, :].reshape(128, 128)
         turned = part.T
@@ -303,11 +320,12 @@
         )
         attn_ref[0, :, j * 128 : (j + 1) * 128] = (num / den).astype(BF16)
 
-    for cp in sends_f:
-        cp.wait()
     piece = kept["own"]
-    for i, j in CHIPS:
-        piece = piece + fr[i, j].astype(F32)
+    for i in range(2):
+        for cp in sends_f[7 * i : 7 + 8 * i]:
+            cp.wait()
+        for j in range(1 - i, 8):
+            piece = piece + fr[i, j].astype(F32)
     ffn_ref[...] = unfold(piece).astype(BF16)
 
 
@@ -335,13 +353,14 @@
             pltpu.VMEM((4, 4, 16, 512), BF16),
             pltpu.VMEM((4, 4, 16, 512), BF16),
             pltpu.VMEM((4, 4, 4, 16, 256), BF16),
-            pltpu.VMEM((2, 64, 512), F32),
+            pltpu.VMEM((64, 512), F32),
             pltpu.VMEM((2, 64, 512), BF16),
             pltpu.VMEM((2, 64, 512), BF16),
             pltpu.VMEM((2, 8, 16, 256), BF16),
             pltpu.VMEM((2, 8, 16, 256), BF16),
-            pltpu.VMEM((16, 32, 128), BF16),
-            pltpu.VMEM((16, 32, 128), BF16),
+            pltpu.VMEM((4, 4, 32, 128), BF16),
+            pltpu.VMEM((4, 4, 32, 128), BF16),
+            pltpu.VMEM((4, 4, 32, 128), BF16),
             dma((6,)),
             dma((2, 8)), dma((2, 8)),
             dma((2,)), dma((2,)),
@@ -350,9 +369,9 @@
             dma((4, 4)), dma((4, 4)),
             dma((4, 4)), dma((4, 4)),
             dma((4, 16)), dma((4, 16)),
-            dma((2,)), dma((2,)),
+            dma((4,)), dma((4,)),
             dma((2, 8)), dma((2, 8)),
-            dma((16,)), dma((16,)),
+            dma((8,)), dma((8,)),
         ],
         compiler_params=pltpu.CompilerParams(
             collective_id=0, has_side_effects=True, vmem_limit_bytes=60 << 20

time: 56.9 us -> 56.1 us (0.986)
  Pallas kernels: 54.9 us -> 54.1 us
    pallas_call x1, Pallas kernels: 54.9 us -> 54.1 us  [shards(): pl.pallas_call(kernel, out_shape=(pltpu.VMEM((1, 16, 512), BF16), pltpu.V...]
where the time goes in v4:
time: 56.1 us; the launch traced here: 55.9 us
  Pallas kernels  54.1 us (96%)
  local copies, waits for them, and re-layouts  1.21 us (2%)
  between operations  0.64 us (1%)
    pallas_call x1, Pallas kernels, shards(): pl.pallas_call(kernel, out_shape=(pltpu.VMEM((1, 16, 512), BF16), pltpu.V...  54.1 us
    unnamed x2, local copies, waits for them, and re-layouts  1.21 us

profile of v4, /device:TPU:1, one launch (start us, length us, event | category | flops | bytes accessed | tf_op | source)
XLA Modules:
  0.0 55.9 jit_solution(12156831414786951878)
XLA Ops:
  0.6 54.1 %decode_step.1 = (bf16[1,16,512]{2,1,0:T(8,128)(2,1)S(1)}, bf16[8,512]{1,0:T(8,128)(2,1)S(1)}) custom-call(bf16[1,16,8192]{2,1,0:T(8,128)(2,1)} %q_hbm.1, bf16[1,512,1024]{2,1,0:T(8,128)(2,1)} %k_hbm.1, bf16[1,512,1024]{2,1,0:T(8,128)(2,1)} %v_hbm.1, s32[1,16]{1,0:T(1,128)} %count_ref.1, s32[1,16]{1,0:T(1,128)} %trim_ref.1, bf16[8,512]{1,0:T(8,128)(2,1)} %rows_ref.1, ...), custom_call_target="tpu_custom_call" | custom-call | tf_op jit(solution)/shard_map/decode_step/pallas_call | solution.py:336
  54.7 0.6 %copy.13 = bf16[1,16,512]{2,1,0:T(8,128)(2,1)} copy(bf16[1,16,512]{2,1,0:T(8,128)(2,1)S(1)} %get-tuple-element.2) | data formatting | bytes 32768
  55.3 0.6 %copy.14 = bf16[8,512]{1,0:T(8,128)(2,1)} copy(bf16[8,512]{1,0:T(8,128)(2,1)S(1)} %get-tuple-element.3) | data formatting | bytes 16384

commit v5 on v4

--- a/solution.py
+++ b/solution.py
@@ -73,7 +73,7 @@
 
     barrier = pltpu.get_barrier_semaphore()
     partners = (
-        [chip(0, j) for j in range(1, 8)] + [chip(1, 0), sibling]
+        [chip(0, 4), chip(1, 0)] + [chip(0, j) for j in (3, 5, 2, 6, 1, 7)] + [sibling]
         + [plane(i, 0) for i in (1, 2, 3)] + [plane(0, j) for j in (1, 2, 3)]
     )
     for to in partners:
@@ -285,8 +285,8 @@
     hz = {0: over_z(0, pz[0])}
     pz[2] = over_x(2, px[2])
     hz[1] = over_z(1, pz[1])
+    pz[3] = over_x(3, px[3])
     hx = {0: gather_z(0, hz[0])}
-    pz[3] = over_x(3, px[3])
     hz[2] = over_z(2, pz[2])
     hx[1] = gather_z(1, hz[1])
     hz[3] = over_z(3, pz[3])

time: 56.1 us -> 55.7 us (level)
  no operation moved by 1% of the time
where the time goes in v5:
time: 55.7 us; the launch traced here: 55.6 us
  Pallas kernels  53.7 us (96%)
  local copies, waits for them, and re-layouts  1.21 us (2%)
  between operations  0.64 us (1%)
    pallas_call x1, Pallas kernels, shards(): pl.pallas_call(kernel, out_shape=(pltpu.VMEM((1, 16, 512), BF16), pltpu.V...  53.7 us
    unnamed x2, local copies, waits for them, and re-layouts  1.21 us

profile of v5, /device:TPU:1, one launch (start us, length us, event | category | flops | bytes accessed | tf_op | source)
XLA Modules:
  0.0 55.6 jit_solution(12534547378084862703)
XLA Ops:
  0.6 53.7 %decode_step.1 = (bf16[1,16,512]{2,1,0:T(8,128)(2,1)S(1)}, bf16[8,512]{1,0:T(8,128)(2,1)S(1)}) custom-call(bf16[1,16,8192]{2,1,0:T(8,128)(2,1)} %q_hbm.1, bf16[1,512,1024]{2,1,0:T(8,128)(2,1)} %k_hbm.1, bf16[1,512,1024]{2,1,0:T(8,128)(2,1)} %v_hbm.1, s32[1,16]{1,0:T(1,128)} %count_ref.1, s32[1,16]{1,0:T(1,128)} %trim_ref.1, bf16[8,512]{1,0:T(8,128)(2,1)} %rows_ref.1, ...), custom_call_target="tpu_custom_call" | custom-call | tf_op jit(solution)/shard_map/decode_step/pallas_call | solution.py:336
  54.4 0.6 %copy.13 = bf16[1,16,512]{2,1,0:T(8,128)(2,1)} copy(bf16[1,16,512]{2,1,0:T(8,128)(2,1)S(1)} %get-tuple-element.2) | data formatting | bytes 32768
  55.0 0.6 %copy.14 = bf16[8,512]{1,0:T(8,128)(2,1)} copy(bf16[8,512]{1,0:T(8,128)(2,1)S(1)} %get-tuple-element.3) | data formatting | bytes 16384
